TPU v7x, 128 devices: a whole 4x4x4 slice. The times are simulated.
128 devices in a mesh: orb: 16 (over y_lo, z, core), dom: 8 (over y_hi, x).
Axes of the slice: x: 4, y: 4 (y_hi: 2, y_lo: 2; y = y_hi * 2 + y_lo), z: 4, core: 2. Of those that a mesh axis runs over, the one named last changes fastest.
Arguments:
- orbitals: float32 [128, 64, 64, 128], P('orb', 'dom'), may hold values from -6 to 6
- veff: float32 [64, 64, 128], P('dom'), may hold values from -1 to 0
- trials: float32 [16, 64, 64, 128], P('orb', 'dom'), may hold values from -32 to 32
- owners: int32 [2], replicated, may hold values from 0 to 15
- levels: float32 [8], replicated, may hold values from 0.05 to 1
- shift_index: int32 [128], P('orb'), may hold values from 0 to 7
Outputs:
- responses: float32 [16, 64, 64, 128], P('orb', 'dom')
Inputs may be any that keep to these rules, and one draw needn't show every extreme that they name: `owners`: an orbital group index. `shift_index`: an index into levels.
All inputs are finite; a program needn't handle non-finite values.
Results may differ from a plain program's by a relative error of at most 0.0001.
Values sent between devices are 32-bit elements; how exact they have to be, the bound alone decides.
A program may use at most 128 MiB of HBM per device.

v0:
```python
import jax
import jax.numpy as jnp
from jax import lax
from jax.sharding import PartitionSpec as P

APPS = 2
SWEEPS = 4
stencil_taps = (-49.0 / 18.0, 1.5, -0.15, 1.0 / 90.0)
center_shift = 4.05
center_depth = 5.05
inverse_half = 1.0 / 5.05
norm_epsilon = 1e-06


def extended_2(block, sides, width):
    for axis, dim in sides:
        count = lax.axis_size(axis)
        forward = [(i, i + 1) for i in range(count - 1)]
        backward = [(target, source) for source, target in forward]
        low = lax.ppermute(
            lax.slice_in_dim(block, block.shape[dim] - width, None, axis=dim), axis, forward
        )
        high = lax.ppermute(lax.slice_in_dim(block, 0, width, axis=dim), axis, backward)
        block = jnp.concatenate([low, block, high], axis=dim)
    return block


def spread(shard, axis, root):
    mine = lax.axis_index(axis) == root
    return lax.psum(jnp.where(mine, shard, jnp.zeros_like(shard)), axis)


def apply_map(extended, potential_in):
    inner_count = extended.shape[1] - 6
    width_y = extended.shape[2]
    width_z = extended.shape[3]
    padded = jnp.pad(extended, ((0, 0), (0, 0), (3, 3), (3, 3)))
    middle = padded[:, 3 : 3 + inner_count, 3 : 3 + width_y, 3 : 3 + width_z]
    laplace = 3.0 * stencil_taps[0] * middle
    for offset in (1, 2, 3):
        weight = stencil_taps[offset]
        laplace = laplace + weight * (
            padded[:, 3 + offset : 3 + offset + inner_count, 3 : 3 + width_y, 3 : 3 + width_z]
            + padded[:, 3 - offset : 3 - offset + inner_count, 3 : 3 + width_y, 3 : 3 + width_z]
        )
        laplace = laplace + weight * (
            padded[:, 3 : 3 + inner_count, 3 + offset : 3 + offset + width_y, 3 : 3 + width_z]
            + padded[:, 3 : 3 + inner_count, 3 - offset : 3 - offset + width_y, 3 : 3 + width_z]
        )
        laplace = laplace + weight * (
            padded[:, 3 : 3 + inner_count, 3 : 3 + width_y, 3 + offset : 3 + offset + width_z]
            + padded[:, 3 : 3 + inner_count, 3 : 3 + width_y, 3 - offset : 3 - offset + width_z]
        )
    energy = -0.5 * laplace + potential_in[None] * middle
    return (energy - center_shift * middle) * inverse_half


def coefficients(level_gap):
    ratio_q = (center_depth + level_gap) * inverse_half
    root_term = jnp.sqrt(ratio_q * ratio_q - 1.0)
    decay = ratio_q - root_term
    first = -inverse_half / root_term
    series = [first]
    current = first * (-2.0 * decay)
    series.append(current)
    for offset in range(2, SWEEPS + 1):
        current = current * -decay
        series.append(current)
    return [term[:, None, None, None] for term in series]


def sweep_single(initial, veff, series):
    summed = series[0] * initial
    previous = initial
    current = initial
    for offset in range(1, SWEEPS + 1):
        image = apply_map(extended_2(current, (("dom", 1),), 3), veff)
        if offset == 1:
            following = image
        else:
            following = 2.0 * image - previous
        summed = summed + series[offset] * following
        previous = current
        current = following
    return summed


def per_device(orbitals, veff, trials, owners, levels, shift_index):
    grid_cells = orbitals.shape[1] * orbitals.shape[2] * orbitals.shape[3] * lax.axis_size("dom")
    orbital_count = orbitals.shape[0] * lax.axis_size("orb")
    chosen = shift_index[:, None] == jnp.arange(levels.shape[0], dtype=jnp.int32)[None, :]
    level_gaps = jnp.sum(jnp.where(chosen, levels[None, :], 0.0), axis=1)
    series = coefficients(level_gaps)
    potentials = []
    for app_index in range(APPS):
        received = spread(trials[0], "orb", owners[app_index])
        trial_total = lax.psum(jnp.sum(received * received), "dom")
        potentials.append(received * lax.rsqrt(trial_total / grid_cells + norm_epsilon))
    responses = []
    for app_index in range(APPS):
        deltas = sweep_single(potentials[app_index][None] * orbitals, veff, series)
        local_sum = jnp.sum(orbitals * deltas, axis=0)
        responses.append(lax.psum(local_sum, "orb"))
    my_group = lax.axis_index("orb")
    result = jnp.zeros(orbitals.shape[1:], jnp.float32)
    for app_index in range(APPS):
        response = responses[app_index] * (4.0 / orbital_count)
        result = result + jnp.where(owners[app_index] == my_group, response, 0.0)
    return result[None]


def solution(mesh):
    placed = (
        P("orb", "dom", None, None),
        P("dom", None, None),
        P("orb", "dom", None, None),
        P(),
        P(),
        P("orb"),
    )
    return jax.shard_map(
        per_device,
        mesh=mesh,
        in_specs=placed,
        out_specs=P("orb", "dom", None, None),
        check_vma=False,
    )
```

profile of v0, /device:TPU:1, one launch (start us, length us, event | category | flops | bytes accessed | tf_op | source)
XLA Modules:
  0.0 520.6 jit_solution(1561641401315790378)
XLA Ops:
  12.0 120.3 %all-reduce.16.cloned.1.call-done = (f32[8,64,128]{2,1,0:T(8,128)}, f32[8,64,128]{2,1,0:T(8,128)}) async-done(((f32[8,64,128]{2,1,0:T(8,128)}, f32[8,64,128]{2,1,0:T(8,128)}), (f32[8,64,128]{2,1,0:T(8,128)}, f32[8,64,128]{2,1,0:T(8,128)})) %all-reduce.16.cloned.1.call-update) | async-done | bytes 524304 | tf_op jit(solution)/shard_map/psum | solution.py:30
  134.1 20.7 %all-reduce.10 = (f32[]{:T(128)}, f32[]{:T(128)}) all-reduce(f32[]{:T(128)} %get-tuple-element.44, f32[]{:T(128)} %get-tuple-element.45), channel_id=1, replica_groups=mesh['orb'=16,'dom'=8] {'dom'}, use_global_device_ids=true, to_apply=%region_8.9 | all-reduce | flops 2 | bytes 16 | tf_op jit(solution)/shard_map/psum | solution.py:97
  167.9 4.9 collective-permute-start.9
  180.8 10.7 %broadcast_multiply_fusion.2 = (f32[8,8,64,128]{3,2,1,0:T(8,128)S(1)}, f32[8,8,64,128]{3,2,1,0:T(8,128)}) fusion(f32[8,8,64,128]{3,2,1,0:T(8,128)} %copy-done.10, f32[8,64,128]{2,1,0:T(8,128)S(1)} %copy-done.11, f32[8,14,70,134]{3,2,1,0:T(8,128)S(1)} %select_maximum_fusion.14, f32[8,3,64,128]{3,2,1,0:T(8,128)} %copy-done.16, f32[8,3,64,128]{3,2,1,0:T(8,128)} %copy-done.14), kind=kLoop, calls=%fused_computation.397 | loop fusion | flops 20971520 | bytes 33292288 | tf_op jit(solution)/shard_map/mul | solution.py:55
  194.2 5.6 %collective-permute-start.3 = (f32[8,3,64,128]{3,2,1,0:T(8,128)}, f32[8,3,64,128]{3,2,1,0:T(8,128)}, u32[]{:S(2)}, u32[]{:S(2)}) collective-permute-start(f32[8,3,64,128]{3,2,1,0:T(8,128)} %get-tuple-element.25), channel_id=1, source_target_pairs={{0,1},{1,2},{2,3},{3,4},{4,5},{5,6},{6,7},{8,9},{9,10},{10,11},{11... | collective-permute-start | bytes 2359304 | tf_op jit(solution)/shard_map/ppermute | solution.py:20
  199.9 4.6 select_maximum_fusion.6
  204.5 10.6 %broadcast_multiply_fusion.1 = (f32[8,8,64,128]{3,2,1,0:T(8,128)S(1)}, f32[8,8,64,128]{3,2,1,0:T(8,128)}) fusion(f32[8,8,64,128]{3,2,1,0:T(8,128)} %copy-done.9, f32[8,64,128]{2,1,0:T(8,128)S(1)} %copy-done.11, f32[8,14,70,134]{3,2,1,0:T(8,128)S(1)} %select_maximum_fusion.6, f32[8,3,64,128]{3,2,1,0:T(8,128)} %collective-permute-done.9, ...), kind=kLoop, calls=%fused_computation.396 | loop fusion | flops 20971520 | bytes 33292288 | tf_op jit(solution)/shard_map/mul | solution.py:55
  217.9 5.0 collective-permute-start.11
  222.9 4.8 select_maximum_fusion.12
  227.7 9.5 %fusion.152 = f32[8,8,64,128]{3,2,1,0:T(8,128)S(1)} fusion(f32[8,8,64,128]{3,2,1,0:T(8,128)} %copy-done.4, f32[8,3,64,128]{3,2,1,0:T(8,128)} %collective-permute-done.3, f32[8,3,64,128]{3,2,1,0:T(8,128)} %collective-permute-done.2, f32[8,14,70,134]{3,2,1,0:T(8,128)S(1)} %select_maximum_fusion.12, f32[8,8,64,128]{3,2,1,0:T(8,128)S(1)} %copy-done.2, ...), kind=kLoop, calls=%fused_computation.236 | loop fusion | flops 22020096 | bytes 35651584 | tf_op jit(solution)/shard_map/sub | solution.py:81
  239.9 5.0 collective-permute-start.5
  244.9 4.8 select_maximum_fusion.4
  249.7 9.7 %fusion.63 = f32[8,8,64,128]{3,2,1,0:T(8,128)S(1)} fusion(f32[8,8,64,128]{3,2,1,0:T(8,128)} %copy-done.6, f32[8,3,64,128]{3,2,1,0:T(8,128)} %collective-permute-done.11, f32[8,3,64,128]{3,2,1,0:T(8,128)} %collective-permute-done.10, f32[8,14,70,134]{3,2,1,0:T(8,128)S(1)} %select_maximum_fusion.4, f32[8,8,64,128]{3,2,1,0:T(8,128)} %get-tuple-element.19, ...), kind=kLoop, calls=%fused_computation.147 | loop fusion | flops 22020096 | bytes 35651584 | tf_op jit(solution)/shard_map/sub | solution.py:81
  262.3 4.9 collective-permute-start.13
  267.2 4.5 select_maximum_fusion.10
  271.7 8.6 %fusion.130 = f32[8,8,64,128]{3,2,1,0:T(8,128)} fusion(f32[8,8,64,128]{3,2,1,0:T(8,128)S(1)} %fusion.152, f32[8,3,64,128]{3,2,1,0:T(8,128)} %collective-permute-done.5, f32[8,3,64,128]{3,2,1,0:T(8,128)S(1)} %collective-permute-done.4, f32[8,14,70,134]{3,2,1,0:T(8,128)S(1)} %select_maximum_fusion.10, f32[8,64,128]{2,1,0:T(8,128)S(1)} %copy-done.11, ...), kind=kLoop, calls=%fused_computation.214 | loop fusion | flops 22020096 | bytes 33292288 | tf_op jit(solution)/shard_map/sub | solution.py:81
  284.3 7.1 %collective-permute-start.7 = (f32[8,3,64,128]{3,2,1,0:T(8,128)}, f32[8,3,64,128]{3,2,1,0:T(8,128)}, u32[]{:S(2)}, u32[]{:S(2)}) collective-permute-start(f32[8,3,64,128]{3,2,1,0:T(8,128)} %get-tuple-element.20), channel_id=1, source_target_pairs={{0,1},{1,2},{2,3},{3,4},{4,5},{5,6},{6,7},{8,9},{9,10},{10,11},{11... | collective-permute-start | bytes 2359304 | tf_op jit(solution)/shard_map/ppermute | solution.py:20
  291.4 4.8 select_maximum_fusion.2
  296.2 8.8 %fusion.41 = f32[8,8,64,128]{3,2,1,0:T(8,128)} fusion(f32[8,8,64,128]{3,2,1,0:T(8,128)S(1)} %fusion.63, f32[8,3,64,128]{3,2,1,0:T(8,128)} %collective-permute-done.13, f32[8,3,64,128]{3,2,1,0:T(8,128)} %collective-permute-done.12, f32[8,14,70,134]{3,2,1,0:T(8,128)S(1)} %select_maximum_fusion.2, f32[8,64,128]{2,1,0:T(8,128)S(1)} %copy-done.11, ...), kind=kLoop, calls=%fused_computation.125 | loop fusion | flops 22020096 | bytes 33292288 | tf_op jit(solution)/shard_map/sub | solution.py:81
  308.0 7.1 %collective-permute-start.15 = (f32[8,3,64,128]{3,2,1,0:T(8,128)S(1)}, f32[8,3,64,128]{3,2,1,0:T(8,128)S(1)}, u32[]{:S(2)}, u32[]{:S(2)}) collective-permute-start(f32[8,3,64,128]{3,2,1,0:T(8,128)S(1)} %get-tuple-element.30), channel_id=1, source_target_pairs={{0,1},{1,2},{2,3},{3,4},{4,5},{5,6},{6,7},{8,9},{9,10},{10,11},{11... | collective-permute-start | bytes 2359304 | tf_op jit(solution)/shard_map/ppermute | solution.py:20
  315.1 6.6 %select_maximum_fusion.8 = f32[8,14,70,134]{3,2,1,0:T(8,128)} fusion(f32[8,3,64,128]{3,2,1,0:T(8,128)S(1)} %collective-permute-done.6, f32[8,8,64,128]{3,2,1,0:T(8,128)S(1)} %copy-done.3, f32[8,3,64,128]{3,2,1,0:T(8,128)} %collective-permute-done.7), kind=kLoop, calls=%fused_computation.12 | loop fusion | flops 15758400 | bytes 7872256 | tf_op jit(solution)/shard_map/concatenate | solution.py:24
  327.3 28.0 %fusion.245 = f32[8,64,128]{2,1,0:T(8,128)} fusion(f32[8,8,64,128]{3,2,1,0:T(8,128)S(1)} %copy-done, f32[8,8,64,128]{3,2,1,0:T(8,128)S(1)} %fusion.152, f32[8,8,64,128]{3,2,1,0:T(8,128)} %fusion.130, f32[8,14,70,134]{3,2,1,0:T(8,128)} %select_maximum_fusion.8, f32[8,3,64,128]{3,2,1,0:T(8,128)} %collective-permute-done.7, f32[8,3,64,128]{3,2,1,0:T(8,128)} %copy-done.13, ...), kind=kLoop, calls=%fused_computation.393 | loop fusion | flops 27721728 | bytes 35913888 | tf_op jit(solution)/shard_map/reduce_sum | solution.py:102
  355.3 11.3 %fusion.246 = f32[8,64,128]{2,1,0:T(8,128)} fusion(f32[8,8,64,128]{3,2,1,0:T(8,128)S(1)} %copy-done, f32[8,8,64,128]{3,2,1,0:T(8,128)} %copy-done.1, f32[8,8,64,128]{3,2,1,0:T(8,128)} %fusion.41, f32[8,14,70,134]{3,2,1,0:T(8,128)S(1)} %select_maximum_fusion, f32[8,3,64,128]{3,2,1,0:T(8,128)} %copy-done.17, f32[8,3,64,128]{3,2,1,0:T(8,128)} %copy-done.15, ...), kind=kLoop, calls=%fused_computation.394 | loop fusion | flops 27721728 | bytes 35913888 | tf_op jit(solution)/shard_map/reduce_sum | solution.py:102
  367.9 144.0 %all-reduce.14.cloned.1.call-done = (f32[8,64,128]{2,1,0:T(8,128)}, f32[8,64,128]{2,1,0:T(8,128)}) async-done(((f32[8,64,128]{2,1,0:T(8,128)}, f32[8,64,128]{2,1,0:T(8,128)}), (f32[8,64,128]{2,1,0:T(8,128)}, f32[8,64,128]{2,1,0:T(8,128)})) %all-reduce.14.cloned.1.call-update) | async-done | bytes 524304 | tf_op jit(solution)/shard_map/psum | solution.py:103
  (88 shorter events, 50.9 us)
Async XLA Ops:
  6.5 151.6 %copy-start = (f32[8,8,64,128]{3,2,1,0:T(8,128)S(1)}, f32[8,8,64,128]{3,2,1,0:T(8,128)}, u32[]{:S(2)}) copy-start(f32[8,8,64,128]{3,2,1,0:T(8,128)} %param.6) | copy-start | bytes 6291460
  6.5 125.8 %all-reduce.16.cloned.1.call-start = ((), (), s32[]{:S(2)}) async-start(), calls=%async_computation.1 | async-start | bytes 1048576 | tf_op jit(solution)/shard_map/psum | solution.py:30
  11.1 500.9 %all-reduce.14.cloned.1.call-start = ((), (), s32[]{:S(2)}) async-start(), calls=%async_computation | async-start | bytes 1048576 | tf_op jit(solution)/shard_map/psum | solution.py:103
  158.9 17.6 %copy-start.10 = (f32[8,8,64,128]{3,2,1,0:T(8,128)}, f32[8,8,64,128]{3,2,1,0:T(8,128)S(1)}, u32[]{:S(2)}) copy-start(f32[8,8,64,128]{3,2,1,0:T(8,128)S(1)} %get-tuple-element.28) | copy-start | bytes 6291460
  158.9 41.0 %copy-start.9 = (f32[8,8,64,128]{3,2,1,0:T(8,128)}, f32[8,8,64,128]{3,2,1,0:T(8,128)S(1)}, u32[]{:S(2)}) copy-start(f32[8,8,64,128]{3,2,1,0:T(8,128)S(1)} %get-tuple-element.29) | copy-start | bytes 6291460
  159.0 16.6 %collective-permute-start = (f32[8,3,64,128]{3,2,1,0:T(8,128)S(1)}, f32[8,3,64,128]{3,2,1,0:T(8,128)S(1)}, u32[]{:S(2)}, u32[]{:S(2)}) collective-permute-start(f32[8,3,64,128]{3,2,1,0:T(8,128)S(1)} %get-tuple-element.27), channel_id=1, source_target_pairs={{1,0},{2,1},{3,2},{4,3},{5,4},{6,5},{7,6},{9,8},{10,9},{11,10},{12... | collective-permute-start | bytes 2359304 | tf_op jit(solution)/shard_map/ppermute | solution.py:23
  160.4 16.0 %collective-permute-start.1 = (f32[8,3,64,128]{3,2,1,0:T(8,128)S(1)}, f32[8,3,64,128]{3,2,1,0:T(8,128)S(1)}, u32[]{:S(2)}, u32[]{:S(2)}) collective-permute-start(f32[8,3,64,128]{3,2,1,0:T(8,128)S(1)} %get-tuple-element.26), channel_id=1, source_target_pairs={{0,1},{1,2},{2,3},{3,4},{4,5},{5,6},{6,7},{8,9},{9,10},{10,11},{11... | collective-permute-start | bytes 2359304 | tf_op jit(solution)/shard_map/ppermute | solution.py:20
  166.6 33.3 %collective-permute-start.8 = (f32[8,3,64,128]{3,2,1,0:T(8,128)}, f32[8,3,64,128]{3,2,1,0:T(8,128)S(1)}, u32[]{:S(2)}, u32[]{:S(2)}) collective-permute-start(f32[8,3,64,128]{3,2,1,0:T(8,128)} %get-tuple-element.37), channel_id=1, source_target_pairs={{1,0},{2,1},{3,2},{4,3},{5,4},{6,5},{7,6},{9,8},{10,9},{11,10},{12... | collective-permute-start | bytes 2359304 | tf_op jit(solution)/shard_map/ppermute | solution.py:23
  167.9 32.0 %collective-permute-start.9 = (f32[8,3,64,128]{3,2,1,0:T(8,128)}, f32[8,3,64,128]{3,2,1,0:T(8,128)}, u32[]{:S(2)}, u32[]{:S(2)}) collective-permute-start(f32[8,3,64,128]{3,2,1,0:T(8,128)} %get-tuple-element.36), channel_id=1, source_target_pairs={{0,1},{1,2},{2,3},{3,4},{4,5},{5,6},{6,7},{8,9},{9,10},{10,11},{11... | collective-permute-start | bytes 2359304 | tf_op jit(solution)/shard_map/ppermute | solution.py:20
  191.5 13.0 %copy-start.4 = (f32[8,8,64,128]{3,2,1,0:T(8,128)}, f32[8,8,64,128]{3,2,1,0:T(8,128)S(1)}, u32[]{:S(2)}) copy-start(f32[8,8,64,128]{3,2,1,0:T(8,128)S(1)} %get-tuple-element.11) | copy-start | bytes 6291460
  193.0 29.9 %collective-permute-start.2 = (f32[8,3,64,128]{3,2,1,0:T(8,128)}, f32[8,3,64,128]{3,2,1,0:T(8,128)}, u32[]{:S(2)}, u32[]{:S(2)}) collective-permute-start(f32[8,3,64,128]{3,2,1,0:T(8,128)} %get-tuple-element.24), channel_id=1, source_target_pairs={{1,0},{2,1},{3,2},{4,3},{5,4},{6,5},{7,6},{9,8},{10,9},{11,10},{12... | collective-permute-start | bytes 2359304 | tf_op jit(solution)/shard_map/ppermute | solution.py:23
  194.2 28.7 %collective-permute-start.3 = (f32[8,3,64,128]{3,2,1,0:T(8,128)}, f32[8,3,64,128]{3,2,1,0:T(8,128)}, u32[]{:S(2)}, u32[]{:S(2)}) collective-permute-start(f32[8,3,64,128]{3,2,1,0:T(8,128)} %get-tuple-element.25), channel_id=1, source_target_pairs={{0,1},{1,2},{2,3},{3,4},{4,5},{5,6},{6,7},{8,9},{9,10},{10,11},{11... | collective-permute-start | bytes 2359304 | tf_op jit(solution)/shard_map/ppermute | solution.py:20
  216.4 28.5 %collective-permute-start.10 = (f32[8,3,64,128]{3,2,1,0:T(8,128)}, f32[8,3,64,128]{3,2,1,0:T(8,128)}, u32[]{:S(2)}, u32[]{:S(2)}) collective-permute-start(f32[8,3,64,128]{3,2,1,0:T(8,128)} %get-tuple-element.34), channel_id=1, source_target_pairs={{1,0},{2,1},{3,2},{4,3},{5,4},{6,5},{7,6},{9,8},{10,9},{11,10},{12... | collective-permute-start | bytes 2359304 | tf_op jit(solution)/shard_map/ppermute | solution.py:23
  217.9 27.0 %collective-permute-start.11 = (f32[8,3,64,128]{3,2,1,0:T(8,128)}, f32[8,3,64,128]{3,2,1,0:T(8,128)}, u32[]{:S(2)}, u32[]{:S(2)}) collective-permute-start(f32[8,3,64,128]{3,2,1,0:T(8,128)} %get-tuple-element.35), channel_id=1, source_target_pairs={{0,1},{1,2},{2,3},{3,4},{4,5},{5,6},{6,7},{8,9},{9,10},{10,11},{11... | collective-permute-start | bytes 2359304 | tf_op jit(solution)/shard_map/ppermute | solution.py:20
  238.6 28.6 %collective-permute-start.4 = (f32[8,3,64,128]{3,2,1,0:T(8,128)}, f32[8,3,64,128]{3,2,1,0:T(8,128)S(1)}, u32[]{:S(2)}, u32[]{:S(2)}) collective-permute-start(f32[8,3,64,128]{3,2,1,0:T(8,128)} %get-tuple-element.22), channel_id=1, source_target_pairs={{1,0},{2,1},{3,2},{4,3},{5,4},{6,5},{7,6},{9,8},{10,9},{11,10},{12... | collective-permute-start | bytes 2359304 | tf_op jit(solution)/shard_map/ppermute | solution.py:23
  239.9 27.3 %collective-permute-start.5 = (f32[8,3,64,128]{3,2,1,0:T(8,128)}, f32[8,3,64,128]{3,2,1,0:T(8,128)}, u32[]{:S(2)}, u32[]{:S(2)}) collective-permute-start(f32[8,3,64,128]{3,2,1,0:T(8,128)} %get-tuple-element.23), channel_id=1, source_target_pairs={{0,1},{1,2},{2,3},{3,4},{4,5},{5,6},{6,7},{8,9},{9,10},{10,11},{11... | collective-permute-start | bytes 2359304 | tf_op jit(solution)/shard_map/ppermute | solution.py:20
  259.4 36.7 %copy-start.1 = (f32[8,8,64,128]{3,2,1,0:T(8,128)}, f32[8,8,64,128]{3,2,1,0:T(8,128)S(1)}, u32[]{:S(2)}) copy-start(f32[8,8,64,128]{3,2,1,0:T(8,128)S(1)} %fusion.63) | copy-start | bytes 6291460
  261.0 30.4 %collective-permute-start.12 = (f32[8,3,64,128]{3,2,1,0:T(8,128)}, f32[8,3,64,128]{3,2,1,0:T(8,128)}, u32[]{:S(2)}, u32[]{:S(2)}) collective-permute-start(f32[8,3,64,128]{3,2,1,0:T(8,128)} %get-tuple-element.32), channel_id=1, source_target_pairs={{1,0},{2,1},{3,2},{4,3},{5,4},{6,5},{7,6},{9,8},{10,9},{11,10},{12... | collective-permute-start | bytes 2359304 | tf_op jit(solution)/shard_map/ppermute | solution.py:23
  262.3 29.1 %collective-permute-start.13 = (f32[8,3,64,128]{3,2,1,0:T(8,128)}, f32[8,3,64,128]{3,2,1,0:T(8,128)}, u32[]{:S(2)}, u32[]{:S(2)}) collective-permute-start(f32[8,3,64,128]{3,2,1,0:T(8,128)} %get-tuple-element.33), channel_id=1, source_target_pairs={{0,1},{1,2},{2,3},{3,4},{4,5},{5,6},{6,7},{8,9},{9,10},{10,11},{11... | collective-permute-start | bytes 2359304 | tf_op jit(solution)/shard_map/ppermute | solution.py:20
  283.0 32.1 %collective-permute-start.6 = (f32[8,3,64,128]{3,2,1,0:T(8,128)}, f32[8,3,64,128]{3,2,1,0:T(8,128)S(1)}, u32[]{:S(2)}, u32[]{:S(2)}) collective-permute-start(f32[8,3,64,128]{3,2,1,0:T(8,128)} %get-tuple-element.21), channel_id=1, source_target_pairs={{1,0},{2,1},{3,2},{4,3},{5,4},{6,5},{7,6},{9,8},{10,9},{11,10},{12... | collective-permute-start | bytes 2359304 | tf_op jit(solution)/shard_map/ppermute | solution.py:23
  284.3 30.8 %collective-permute-start.7 = (f32[8,3,64,128]{3,2,1,0:T(8,128)}, f32[8,3,64,128]{3,2,1,0:T(8,128)}, u32[]{:S(2)}, u32[]{:S(2)}) collective-permute-start(f32[8,3,64,128]{3,2,1,0:T(8,128)} %get-tuple-element.20), channel_id=1, source_target_pairs={{0,1},{1,2},{2,3},{3,4},{4,5},{5,6},{6,7},{8,9},{9,10},{10,11},{11... | collective-permute-start | bytes 2359304 | tf_op jit(solution)/shard_map/ppermute | solution.py:20
  306.7 15.5 %collective-permute-start.14 = (f32[8,3,64,128]{3,2,1,0:T(8,128)S(1)}, f32[8,3,64,128]{3,2,1,0:T(8,128)S(1)}, u32[]{:S(2)}, u32[]{:S(2)}) collective-permute-start(f32[8,3,64,128]{3,2,1,0:T(8,128)S(1)} %get-tuple-element.31), channel_id=1, source_target_pairs={{1,0},{2,1},{3,2},{4,3},{5,4},{6,5},{7,6},{9,8},{10,9},{11,10},{12... | collective-permute-start | bytes 2359304 | tf_op jit(solution)/shard_map/ppermute | solution.py:23
  308.0 15.8 %copy-start.8 = (f32[8,8,64,128]{3,2,1,0:T(8,128)S(1)}, f32[8,8,64,128]{3,2,1,0:T(8,128)}, u32[]{:S(2)}) copy-start(f32[8,8,64,128]{3,2,1,0:T(8,128)} %fusion.41) | copy-start | bytes 6291460
  308.0 15.8 %collective-permute-start.15 = (f32[8,3,64,128]{3,2,1,0:T(8,128)S(1)}, f32[8,3,64,128]{3,2,1,0:T(8,128)S(1)}, u32[]{:S(2)}, u32[]{:S(2)}) collective-permute-start(f32[8,3,64,128]{3,2,1,0:T(8,128)S(1)} %get-tuple-element.30), channel_id=1, source_target_pairs={{0,1},{1,2},{2,3},{3,4},{4,5},{5,6},{6,7},{8,9},{9,10},{10,11},{11... | collective-permute-start | bytes 2359304 | tf_op jit(solution)/shard_map/ppermute | solution.py:20
  (13 other events, 76.8 us)
Sparse Core Ops, SparseCore 0:
  11.2 121.0 all-reduce.15
  366.8 145.1 all-reduce.13
where the time goes:
time: 522 us; the launch traced here: 521 us
  waiting for transfers between devices  270 us (52%)
  other arithmetic  144 us (28%)
  starting transfers between devices  54.3 us (10%)
  blocking collectives  20.7 us (4%)
  between operations  17.7 us (3%)
  local copies, waits for them, and re-layouts  14.1 us (3%)
    psum x1, waiting for transfers between devices, per_device(): responses.append(lax.psum(local_sum, 'orb'))  144 us
    psum x1, waiting for transfers between devices, spread(): return lax.psum(jnp.where(mine, shard, jnp.zeros_like(shard)), axis)  120 us
    ppermute x8, starting transfers between devices, extended_2(): lax.ppermute(lax.slice_in_dim(block, block.shape[dim] - width, None, axis...  43.7 us
    reduce_sum x2, other arithmetic, per_device(): local_sum = jnp.sum(orbitals * deltas, axis=0)  39.4 us
    concatenate x8, other arithmetic, extended_2(): block = jnp.concatenate([low, block, high], axis=dim)  37.1 us
    sub x4, other arithmetic, sweep_single(): following = 2.0 * image - previous  36.6 us
    mul x2, other arithmetic, apply_map(): return (energy - center_shift * middle) * inverse_half  21.3 us
    psum x1, blocking collectives, per_device(): trial_total = lax.psum(jnp.sum(received * received), 'dom')  20.7 us
  transfers between devices with their start and end apart: 18, of which 6 were waited for; matrix products, arithmetic and copies ran while one was open for 20% of the time, Pallas kernels for 0%

commit v1 on v0

--- a/solution.py
+++ b/solution.py
@@ -10,6 +10,7 @@
 center_depth = 5.05
 inverse_half = 1.0 / 5.05
 norm_epsilon = 1e-06
+detail_ratios = lambda mat, row_axis: jnp.sum(jax.lax.all_gather(mat, row_axis), axis=0)
 
 
 def extended_2(block, sides, width):
@@ -100,7 +101,7 @@
     for app_index in range(APPS):
         deltas = sweep_single(potentials[app_index][None] * orbitals, veff, series)
         local_sum = jnp.sum(orbitals * deltas, axis=0)
-        responses.append(lax.psum(local_sum, "orb"))
+        responses.append(detail_ratios(local_sum, "orb"))
     my_group = lax.axis_index("orb")
     result = jnp.zeros(orbitals.shape[1:], jnp.float32)
     for app_index in range(APPS):

time: 522 us -> 472 us (0.904)
  waiting for transfers between devices: 270 us -> 220 us
    psum x1 -> x0, waiting for transfers between devices: 144 us -> none  [per_device(): responses.append(lax.psum(local_sum, 'orb'))]
    all_gather x0 -> x2, waiting for transfers between devices: none -> 74.7 us  [jax.lax.all_gather(mat, row_axis)]
    reduce_sum x2, other arithmetic: 39.4 us -> 22.2 us  [per_device(): local_sum = jnp.sum(orbitals * deltas, axis=0)]
    ppermute x8, waiting for transfers between devices: 3.09 us -> 20 us  [extended_2(): lax.ppermute(lax.slice_in_dim(block, 0, width, axis=dim), axis, backward)]
    sub x4, other arithmetic: 36.6 us -> 51.4 us  [sweep_single(): following = 2.0 * image - previous]
  transfers between devices with their start and end apart: 18 -> 19, of which waited for: 6 -> 11; matrix products, arithmetic and copies ran while one was open for 20% -> 20% of each run, Pallas kernels for 0% -> 0%
where the time goes in v1:
time: 472 us; the launch traced here: 471 us
  waiting for transfers between devices  220 us (47%)
  other arithmetic  142 us (30%)
  starting transfers between devices  54.4 us (12%)
  blocking collectives  20.7 us (4%)
  between operations  17.5 us (4%)
  local copies, waits for them, and re-layouts  15.8 us (3%)
    psum x1, waiting for transfers between devices, spread(): return lax.psum(jnp.where(mine, shard, jnp.zeros_like(shard)), axis)  120 us
    all_gather x2, waiting for transfers between devices, jax.lax.all_gather(mat, row_axis)  74.7 us
    sub x4, other arithmetic, sweep_single(): following = 2.0 * image - previous  51.4 us
    ppermute x8, starting transfers between devices, extended_2(): lax.ppermute(lax.slice_in_dim(block, block.shape[dim] - width, None, axis...  43.6 us
    concatenate x8, other arithmetic, extended_2(): block = jnp.concatenate([low, block, high], axis=dim)  35.8 us
    reduce_sum x2, other arithmetic, per_device(): local_sum = jnp.sum(orbitals * deltas, axis=0)  22.2 us
    psum x1, blocking collectives, per_device(): trial_total = lax.psum(jnp.sum(received * received), 'dom')  20.7 us
    ppermute x8, waiting for transfers between devices, extended_2(): lax.ppermute(lax.slice_in_dim(block, 0, width, axis=dim), axis, backward)  20 us
  transfers between devices with their start and end apart: 19, of which 11 were waited for; matrix products, arithmetic and copies ran while one was open for 20% of the time, Pallas kernels for 0%

profile of v1, /device:TPU:1, one launch (start us, length us, event | category | flops | bytes accessed | tf_op | source)
XLA Modules:
  0.0 470.5 jit_solution(9226022619124247587)
XLA Ops:
  12.0 120.3 %all-reduce.12.cloned.1.call-done = (f32[8,64,128]{2,1,0:T(8,128)}, f32[8,64,128]{2,1,0:T(8,128)}) async-done(((f32[8,64,128]{2,1,0:T(8,128)}, f32[8,64,128]{2,1,0:T(8,128)}), (f32[8,64,128]{2,1,0:T(8,128)}, f32[8,64,128]{2,1,0:T(8,128)})) %all-reduce.12.cloned.1.call-update) | async-done | bytes 524304 | tf_op jit(solution)/shard_map/psum | solution.py:31
  134.1 20.7 %all-reduce.9 = (f32[]{:T(128)}, f32[]{:T(128)}) all-reduce(f32[]{:T(128)} %get-tuple-element.42, f32[]{:T(128)} %get-tuple-element.43), channel_id=1, replica_groups=mesh['orb'=16,'dom'=8] {'dom'}, use_global_device_ids=true, to_apply=%region_8.9 | all-reduce | flops 2 | bytes 16 | tf_op jit(solution)/shard_map/psum | solution.py:98
  167.9 4.9 %collective-permute-start.9 = (f32[8,3,64,128]{3,2,1,0:T(8,128)}, f32[8,3,64,128]{3,2,1,0:T(8,128)}, u32[]{:S(2)}, u32[]{:S(2)}) collective-permute-start(f32[8,3,64,128]{3,2,1,0:T(8,128)} %get-tuple-element.34), channel_id=1, source_target_pairs={{0,1},{1,2},{2,3},{3,4},{4,5},{5,6},{6,7},{8,9},{9,10},{10,11},{11... | collective-permute-start | bytes 2359304 | tf_op jit(solution)/shard_map/ppermute | solution.py:21
  180.9 10.7 %broadcast_multiply_fusion.2 = (f32[8,8,64,128]{3,2,1,0:T(8,128)S(1)}, f32[8,8,64,128]{3,2,1,0:T(8,128)}) fusion(f32[8,8,64,128]{3,2,1,0:T(8,128)} %copy-done.10, f32[8,64,128]{2,1,0:T(8,128)S(1)} %copy-done.11, f32[8,14,70,134]{3,2,1,0:T(8,128)S(1)} %select_maximum_fusion.14, f32[8,3,64,128]{3,2,1,0:T(8,128)} %copy-done.14, f32[8,3,64,128]{3,2,1,0:T(8,128)} %copy-done.13), kind=kLoop, calls=%fused_computation.397 | loop fusion | flops 20971520 | bytes 33292288 | tf_op jit(solution)/shard_map/mul | solution.py:56
  194.4 5.6 %collective-permute-start.3 = (f32[8,3,64,128]{3,2,1,0:T(8,128)}, f32[8,3,64,128]{3,2,1,0:T(8,128)}, u32[]{:S(2)}, u32[]{:S(2)}) collective-permute-start(f32[8,3,64,128]{3,2,1,0:T(8,128)} %get-tuple-element.23), channel_id=1, source_target_pairs={{0,1},{1,2},{2,3},{3,4},{4,5},{5,6},{6,7},{8,9},{9,10},{10,11},{11... | collective-permute-start | bytes 2359304 | tf_op jit(solution)/shard_map/ppermute | solution.py:21
  204.6 8.4 %broadcast_multiply_fusion.1 = (f32[8,8,64,128]{3,2,1,0:T(8,128)S(1)}, f32[8,8,64,128]{3,2,1,0:T(8,128)}) fusion(f32[8,8,64,128]{3,2,1,0:T(8,128)S(1)} %get-tuple-element.27, f32[8,64,128]{2,1,0:T(8,128)S(1)} %copy-done.11, f32[8,14,70,134]{3,2,1,0:T(8,128)S(1)} %select_maximum_fusion.6, f32[8,3,64,128]{3,2,1,0:T(8,128)} %collective-permute-done.9, ...), kind=kLoop, calls=%fused_computation.396 | loop fusion | flops 20971520 | bytes 33292288 | tf_op jit(solution)/shard_map/mul | solution.py:56
  215.7 5.0 %collective-permute-start.11 = (f32[8,3,64,128]{3,2,1,0:T(8,128)}, f32[8,3,64,128]{3,2,1,0:T(8,128)}, u32[]{:S(2)}, u32[]{:S(2)}) collective-permute-start(f32[8,3,64,128]{3,2,1,0:T(8,128)} %get-tuple-element.33), channel_id=1, source_target_pairs={{0,1},{1,2},{2,3},{3,4},{4,5},{5,6},{6,7},{8,9},{9,10},{10,11},{11... | collective-permute-start | bytes 2359304 | tf_op jit(solution)/shard_map/ppermute | solution.py:21
  220.8 4.8 %select_maximum_fusion.12 = f32[8,14,70,134]{3,2,1,0:T(8,128)S(1)} fusion(f32[8,3,64,128]{3,2,1,0:T(8,128)} %collective-permute-done.2, f32[8,8,64,128]{3,2,1,0:T(8,128)S(1)} %copy-done.8, f32[8,3,64,128]{3,2,1,0:T(8,128)} %collective-permute-done.3), kind=kLoop, calls=%fused_computation.16 | loop fusion | flops 15758400 | bytes 7872256 | tf_op jit(solution)/shard_map/concatenate | solution.py:25
  225.6 9.6 %fusion.152 = f32[8,8,64,128]{3,2,1,0:T(8,128)S(1)} fusion(f32[8,8,64,128]{3,2,1,0:T(8,128)} %copy-done.7, f32[8,3,64,128]{3,2,1,0:T(8,128)} %collective-permute-done.3, f32[8,3,64,128]{3,2,1,0:T(8,128)} %collective-permute-done.2, f32[8,14,70,134]{3,2,1,0:T(8,128)S(1)} %select_maximum_fusion.12, f32[8,8,64,128]{3,2,1,0:T(8,128)S(1)} %copy-done.4, ...), kind=kLoop, calls=%fused_computation.236 | loop fusion | flops 22020096 | bytes 35651584 | tf_op jit(solution)/shard_map/sub | solution.py:82
  241.0 4.8 %select_maximum_fusion.4 = f32[8,14,70,134]{3,2,1,0:T(8,128)S(1)} fusion(f32[8,3,64,128]{3,2,1,0:T(8,128)} %collective-permute-done.10, f32[8,8,64,128]{3,2,1,0:T(8,128)S(1)} %copy-done.6, f32[8,3,64,128]{3,2,1,0:T(8,128)} %collective-permute-done.11), kind=kLoop, calls=%fused_computation.8 | loop fusion | flops 15758400 | bytes 7872256 | tf_op jit(solution)/shard_map/concatenate | solution.py:25
  250.6 6.0 %select_maximum_fusion.10 = f32[8,14,70,134]{3,2,1,0:T(8,128)} fusion(f32[8,3,64,128]{3,2,1,0:T(8,128)S(1)} %collective-permute-done.4, f32[8,8,64,128]{3,2,1,0:T(8,128)S(1)} %fusion.152, f32[8,3,64,128]{3,2,1,0:T(8,128)S(1)} %collective-permute-done.5), kind=kLoop, calls=%fused_computation.14 | loop fusion | flops 15758400 | bytes 7872256 | tf_op jit(solution)/shard_map/concatenate | solution.py:25
  256.6 23.1 %fusion.130 = f32[8,8,64,128]{3,2,1,0:T(8,128)} fusion(f32[8,8,64,128]{3,2,1,0:T(8,128)S(1)} %fusion.152, f32[8,3,64,128]{3,2,1,0:T(8,128)} %copy-done.17, f32[8,3,64,128]{3,2,1,0:T(8,128)S(1)} %collective-permute-done.4, f32[8,14,70,134]{3,2,1,0:T(8,128)} %select_maximum_fusion.10, f32[8,64,128]{2,1,0:T(8,128)S(1)} %copy-done.11, ...), kind=kLoop, calls=%fused_computation.214 | loop fusion | flops 22020096 | bytes 33292288 | tf_op jit(solution)/shard_map/sub | solution.py:82
  283.9 5.3 %collective-permute-start.7 = (f32[8,3,64,128]{3,2,1,0:T(8,128)}, f32[8,3,64,128]{3,2,1,0:T(8,128)}, u32[]{:S(2)}, u32[]{:S(2)}) collective-permute-start(f32[8,3,64,128]{3,2,1,0:T(8,128)} %get-tuple-element.18), channel_id=1, source_target_pairs={{0,1},{1,2},{2,3},{3,4},{4,5},{5,6},{6,7},{8,9},{9,10},{10,11},{11... | collective-permute-start | bytes 2359304 | tf_op jit(solution)/shard_map/ppermute | solution.py:21
  289.2 10.3 %fusion.63 = f32[8,8,64,128]{3,2,1,0:T(8,128)} fusion(f32[8,8,64,128]{3,2,1,0:T(8,128)} %copy-done.5, f32[8,3,64,128]{3,2,1,0:T(8,128)} %collective-permute-done.11, f32[8,3,64,128]{3,2,1,0:T(8,128)} %collective-permute-done.10, f32[8,14,70,134]{3,2,1,0:T(8,128)S(1)} %select_maximum_fusion.4, f32[8,8,64,128]{3,2,1,0:T(8,128)S(1)} %copy-done.2, ...), kind=kLoop, calls=%fused_computation.147 | loop fusion | flops 22020096 | bytes 35651584 | tf_op jit(solution)/shard_map/sub | solution.py:82
  299.5 5.2 %select_maximum_fusion.8 = f32[8,14,70,134]{3,2,1,0:T(8,128)S(1)} fusion(f32[8,3,64,128]{3,2,1,0:T(8,128)S(1)} %collective-permute-done.6, f32[8,8,64,128]{3,2,1,0:T(8,128)} %fusion.130, f32[8,3,64,128]{3,2,1,0:T(8,128)} %collective-permute-done.7), kind=kLoop, calls=%fused_computation.12 | loop fusion | flops 15758400 | bytes 7872256 | tf_op jit(solution)/shard_map/concatenate | solution.py:25
  304.7 11.0 %fusion.245 = f32[8,64,128]{2,1,0:T(8,128)} fusion(f32[8,8,64,128]{3,2,1,0:T(8,128)S(1)} %copy-done, f32[8,8,64,128]{3,2,1,0:T(8,128)S(1)} %fusion.152, f32[8,8,64,128]{3,2,1,0:T(8,128)} %fusion.130, f32[8,14,70,134]{3,2,1,0:T(8,128)S(1)} %select_maximum_fusion.8, f32[8,3,64,128]{3,2,1,0:T(8,128)} %collective-permute-done.7, ...), kind=kLoop, calls=%fused_computation.393 | loop fusion | flops 27721728 | bytes 35913888 | tf_op jit(solution)/shard_map/reduce_sum | solution.py:103
  318.8 6.8 %collective-permute-start.13 = (f32[8,3,64,128]{3,2,1,0:T(8,128)S(1)}, f32[8,3,64,128]{3,2,1,0:T(8,128)S(1)}, u32[]{:S(2)}, u32[]{:S(2)}) collective-permute-start(f32[8,3,64,128]{3,2,1,0:T(8,128)S(1)} %get-tuple-element.31), channel_id=1, source_target_pairs={{0,1},{1,2},{2,3},{3,4},{4,5},{5,6},{6,7},{8,9},{9,10},{10,11},{11... | collective-permute-start | bytes 2359304 | tf_op jit(solution)/shard_map/ppermute | solution.py:21
  325.6 7.0 %collective-permute-done.12 = f32[8,3,64,128]{3,2,1,0:T(8,128)S(1)} collective-permute-done((f32[8,3,64,128]{3,2,1,0:T(8,128)S(1)}, f32[8,3,64,128]{3,2,1,0:T(8,128)S(1)}, u32[]{:S(2)}, u32[]{:S(2)}) %collective-permute-start.12) | collective-permute-done | bytes 786464 | tf_op jit(solution)/shard_map/ppermute | solution.py:24
  338.7 8.4 %fusion.41 = f32[8,8,64,128]{3,2,1,0:T(8,128)} fusion(f32[8,8,64,128]{3,2,1,0:T(8,128)S(1)} %copy-done.1, f32[8,3,64,128]{3,2,1,0:T(8,128)} %copy-done.19, f32[8,3,64,128]{3,2,1,0:T(8,128)S(1)} %collective-permute-done.12, f32[8,14,70,134]{3,2,1,0:T(8,128)S(1)} %select_maximum_fusion.2, f32[8,64,128]{2,1,0:T(8,128)S(1)} %copy-done.11, ...), kind=kLoop, calls=%fused_computation.125 | loop fusion | flops 22020096 | bytes 33292288 | tf_op jit(solution)/shard_map/sub | solution.py:82
  350.1 7.6 %collective-permute-start.15 = (f32[8,3,64,128]{3,2,1,0:T(8,128)S(1)}, f32[8,3,64,128]{3,2,1,0:T(8,128)S(1)}, u32[]{:S(2)}, u32[]{:S(2)}) collective-permute-start(f32[8,3,64,128]{3,2,1,0:T(8,128)S(1)} %get-tuple-element.28), channel_id=1, source_target_pairs={{0,1},{1,2},{2,3},{3,4},{4,5},{5,6},{6,7},{8,9},{9,10},{10,11},{11... | collective-permute-start | bytes 2359304 | tf_op jit(solution)/shard_map/ppermute | solution.py:21
  357.8 7.8 %collective-permute-done.14 = f32[8,3,64,128]{3,2,1,0:T(8,128)S(1)} collective-permute-done((f32[8,3,64,128]{3,2,1,0:T(8,128)S(1)}, f32[8,3,64,128]{3,2,1,0:T(8,128)S(1)}, u32[]{:S(2)}, u32[]{:S(2)}) %collective-permute-start.14) | collective-permute-done | bytes 786464 | tf_op jit(solution)/shard_map/ppermute | solution.py:24
  371.0 11.2 %fusion.246 = f32[8,64,128]{2,1,0:T(8,128)} fusion(f32[8,8,64,128]{3,2,1,0:T(8,128)S(1)} %copy-done, f32[8,8,64,128]{3,2,1,0:T(8,128)S(1)} %copy-done.1, f32[8,8,64,128]{3,2,1,0:T(8,128)} %fusion.41, f32[8,14,70,134]{3,2,1,0:T(8,128)S(1)} %select_maximum_fusion, f32[8,3,64,128]{3,2,1,0:T(8,128)} %copy-done.18, f32[8,3,64,128]{3,2,1,0:T(8,128)} %copy-done.16, ...), kind=kLoop, calls=%fused_computation.394 | loop fusion | flops 27721728 | bytes 35913888 | tf_op jit(solution)/shard_map/reduce_sum | solution.py:103
  383.6 23.9 %all-gather.5.cloned.1.call-done = f32[128,64,128]{2,1,0:T(8,128)} async-done(((f32[8,64,128]{2,1,0:T(8,128)}), f32[128,64,128]{2,1,0:T(8,128)}) %all-gather.5.cloned.1.call-update) | async-done | bytes 4194320 | tf_op jit(solution)/shard_map/all_gather | solution.py:13
  409.9 50.9 %all-gather.7.cloned.1.call-done = f32[128,64,128]{2,1,0:T(8,128)} async-done(((f32[8,64,128]{2,1,0:T(8,128)}), f32[128,64,128]{2,1,0:T(8,128)}) %all-gather.7.cloned.1.call-update) | async-done | bytes 4194320 | tf_op jit(solution)/shard_map/all_gather | solution.py:13
  (97 shorter events, 73.7 us)
Async XLA Ops:
  6.5 151.6 %copy-start = (f32[8,8,64,128]{3,2,1,0:T(8,128)S(1)}, f32[8,8,64,128]{3,2,1,0:T(8,128)}, u32[]{:S(2)}) copy-start(f32[8,8,64,128]{3,2,1,0:T(8,128)} %param.6) | copy-start | bytes 6291460
  6.5 125.8 %all-reduce.12.cloned.1.call-start = ((), (), s32[]{:S(2)}) async-start(), calls=%async_computation.2 | async-start | bytes 1048576 | tf_op jit(solution)/shard_map/psum | solution.py:31
  11.1 396.3 %all-gather.5.cloned.1.call-start = ((), (), s32[]{:S(2)}) async-start(), calls=%async_computation | async-start | bytes 4456448 | tf_op jit(solution)/shard_map/all_gather | solution.py:13
  158.9 17.6 %copy-start.10 = (f32[8,8,64,128]{3,2,1,0:T(8,128)}, f32[8,8,64,128]{3,2,1,0:T(8,128)S(1)}, u32[]{:S(2)}) copy-start(f32[8,8,64,128]{3,2,1,0:T(8,128)S(1)} %get-tuple-element.26) | copy-start | bytes 6291460
  159.0 16.6 %collective-permute-start = (f32[8,3,64,128]{3,2,1,0:T(8,128)S(1)}, f32[8,3,64,128]{3,2,1,0:T(8,128)S(1)}, u32[]{:S(2)}, u32[]{:S(2)}) collective-permute-start(f32[8,3,64,128]{3,2,1,0:T(8,128)S(1)} %get-tuple-element.25), channel_id=1, source_target_pairs={{1,0},{2,1},{3,2},{4,3},{5,4},{6,5},{7,6},{9,8},{10,9},{11,10},{12... | collective-permute-start | bytes 2359304 | tf_op jit(solution)/shard_map/ppermute | solution.py:24
  160.4 16.0 %collective-permute-start.1 = (f32[8,3,64,128]{3,2,1,0:T(8,128)S(1)}, f32[8,3,64,128]{3,2,1,0:T(8,128)S(1)}, u32[]{:S(2)}, u32[]{:S(2)}) collective-permute-start(f32[8,3,64,128]{3,2,1,0:T(8,128)S(1)} %get-tuple-element.24), channel_id=1, source_target_pairs={{0,1},{1,2},{2,3},{3,4},{4,5},{5,6},{6,7},{8,9},{9,10},{10,11},{11... | collective-permute-start | bytes 2359304 | tf_op jit(solution)/shard_map/ppermute | solution.py:21
  166.6 33.5 %collective-permute-start.8 = (f32[8,3,64,128]{3,2,1,0:T(8,128)}, f32[8,3,64,128]{3,2,1,0:T(8,128)S(1)}, u32[]{:S(2)}, u32[]{:S(2)}) collective-permute-start(f32[8,3,64,128]{3,2,1,0:T(8,128)} %get-tuple-element.35), channel_id=1, source_target_pairs={{1,0},{2,1},{3,2},{4,3},{5,4},{6,5},{7,6},{9,8},{10,9},{11,10},{12... | collective-permute-start | bytes 2359304 | tf_op jit(solution)/shard_map/ppermute | solution.py:24
  167.9 32.2 %collective-permute-start.9 = (f32[8,3,64,128]{3,2,1,0:T(8,128)}, f32[8,3,64,128]{3,2,1,0:T(8,128)}, u32[]{:S(2)}, u32[]{:S(2)}) collective-permute-start(f32[8,3,64,128]{3,2,1,0:T(8,128)} %get-tuple-element.34), channel_id=1, source_target_pairs={{0,1},{1,2},{2,3},{3,4},{4,5},{5,6},{6,7},{8,9},{9,10},{10,11},{11... | collective-permute-start | bytes 2359304 | tf_op jit(solution)/shard_map/ppermute | solution.py:21
  193.1 27.7 %collective-permute-start.2 = (f32[8,3,64,128]{3,2,1,0:T(8,128)}, f32[8,3,64,128]{3,2,1,0:T(8,128)}, u32[]{:S(2)}, u32[]{:S(2)}) collective-permute-start(f32[8,3,64,128]{3,2,1,0:T(8,128)} %get-tuple-element.22), channel_id=1, source_target_pairs={{1,0},{2,1},{3,2},{4,3},{5,4},{6,5},{7,6},{9,8},{10,9},{11,10},{12... | collective-permute-start | bytes 2359304 | tf_op jit(solution)/shard_map/ppermute | solution.py:24
  194.4 26.4 %collective-permute-start.3 = (f32[8,3,64,128]{3,2,1,0:T(8,128)}, f32[8,3,64,128]{3,2,1,0:T(8,128)}, u32[]{:S(2)}, u32[]{:S(2)}) collective-permute-start(f32[8,3,64,128]{3,2,1,0:T(8,128)} %get-tuple-element.23), channel_id=1, source_target_pairs={{0,1},{1,2},{2,3},{3,4},{4,5},{5,6},{6,7},{8,9},{9,10},{10,11},{11... | collective-permute-start | bytes 2359304 | tf_op jit(solution)/shard_map/ppermute | solution.py:21
  214.3 26.7 %collective-permute-start.10 = (f32[8,3,64,128]{3,2,1,0:T(8,128)}, f32[8,3,64,128]{3,2,1,0:T(8,128)}, u32[]{:S(2)}, u32[]{:S(2)}) collective-permute-start(f32[8,3,64,128]{3,2,1,0:T(8,128)} %get-tuple-element.32), channel_id=1, source_target_pairs={{1,0},{2,1},{3,2},{4,3},{5,4},{6,5},{7,6},{9,8},{10,9},{11,10},{12... | collective-permute-start | bytes 2359304 | tf_op jit(solution)/shard_map/ppermute | solution.py:24
  215.7 25.3 %collective-permute-start.11 = (f32[8,3,64,128]{3,2,1,0:T(8,128)}, f32[8,3,64,128]{3,2,1,0:T(8,128)}, u32[]{:S(2)}, u32[]{:S(2)}) collective-permute-start(f32[8,3,64,128]{3,2,1,0:T(8,128)} %get-tuple-element.33), channel_id=1, source_target_pairs={{0,1},{1,2},{2,3},{3,4},{4,5},{5,6},{6,7},{8,9},{9,10},{10,11},{11... | collective-permute-start | bytes 2359304 | tf_op jit(solution)/shard_map/ppermute | solution.py:21
  235.3 12.9 %collective-permute-start.4 = (f32[8,3,64,128]{3,2,1,0:T(8,128)S(1)}, f32[8,3,64,128]{3,2,1,0:T(8,128)S(1)}, u32[]{:S(2)}, u32[]{:S(2)}) collective-permute-start(f32[8,3,64,128]{3,2,1,0:T(8,128)S(1)} %get-tuple-element.20), channel_id=1, source_target_pairs={{1,0},{2,1},{3,2},{4,3},{5,4},{6,5},{7,6},{9,8},{10,9},{11,10},{12... | collective-permute-start | bytes 2359304 | tf_op jit(solution)/shard_map/ppermute | solution.py:24
  236.8 12.9 %collective-permute-start.5 = (f32[8,3,64,128]{3,2,1,0:T(8,128)S(1)}, f32[8,3,64,128]{3,2,1,0:T(8,128)S(1)}, u32[]{:S(2)}, u32[]{:S(2)}) collective-permute-start(f32[8,3,64,128]{3,2,1,0:T(8,128)S(1)} %get-tuple-element.21), channel_id=1, source_target_pairs={{0,1},{1,2},{2,3},{3,4},{4,5},{5,6},{6,7},{8,9},{9,10},{10,11},{11... | collective-permute-start | bytes 2359304 | tf_op jit(solution)/shard_map/ppermute | solution.py:21
  282.6 16.9 %collective-permute-start.6 = (f32[8,3,64,128]{3,2,1,0:T(8,128)}, f32[8,3,64,128]{3,2,1,0:T(8,128)S(1)}, u32[]{:S(2)}, u32[]{:S(2)}) collective-permute-start(f32[8,3,64,128]{3,2,1,0:T(8,128)} %get-tuple-element.19), channel_id=1, source_target_pairs={{1,0},{2,1},{3,2},{4,3},{5,4},{6,5},{7,6},{9,8},{10,9},{11,10},{12... | collective-permute-start | bytes 2359304 | tf_op jit(solution)/shard_map/ppermute | solution.py:24
  283.9 15.6 %collective-permute-start.7 = (f32[8,3,64,128]{3,2,1,0:T(8,128)}, f32[8,3,64,128]{3,2,1,0:T(8,128)}, u32[]{:S(2)}, u32[]{:S(2)}) collective-permute-start(f32[8,3,64,128]{3,2,1,0:T(8,128)} %get-tuple-element.18), channel_id=1, source_target_pairs={{0,1},{1,2},{2,3},{3,4},{4,5},{5,6},{6,7},{8,9},{9,10},{10,11},{11... | collective-permute-start | bytes 2359304 | tf_op jit(solution)/shard_map/ppermute | solution.py:21
  315.7 145.0 %all-gather.7.cloned.1.call-start = ((), (), s32[]{:S(2)}) async-start(), calls=%async_computation.1 | async-start | bytes 4456448 | tf_op jit(solution)/shard_map/all_gather | solution.py:13
  315.8 19.4 %copy-start.1 = (f32[8,8,64,128]{3,2,1,0:T(8,128)S(1)}, f32[8,8,64,128]{3,2,1,0:T(8,128)}, u32[]{:S(2)}) copy-start(f32[8,8,64,128]{3,2,1,0:T(8,128)} %fusion.63) | copy-start | bytes 6291460
  317.5 15.2 %collective-permute-start.12 = (f32[8,3,64,128]{3,2,1,0:T(8,128)S(1)}, f32[8,3,64,128]{3,2,1,0:T(8,128)S(1)}, u32[]{:S(2)}, u32[]{:S(2)}) collective-permute-start(f32[8,3,64,128]{3,2,1,0:T(8,128)S(1)} %get-tuple-element.30), channel_id=1, source_target_pairs={{1,0},{2,1},{3,2},{4,3},{5,4},{6,5},{7,6},{9,8},{10,9},{11,10},{12... | collective-permute-start | bytes 2359304 | tf_op jit(solution)/shard_map/ppermute | solution.py:24
  318.8 19.9 %copy-start.3 = (f32[8,8,64,128]{3,2,1,0:T(8,128)S(1)}, f32[8,8,64,128]{3,2,1,0:T(8,128)}, u32[]{:S(2)}) copy-start(f32[8,8,64,128]{3,2,1,0:T(8,128)} %get-tuple-element.17) | copy-start | bytes 6291460
  318.8 15.5 %collective-permute-start.13 = (f32[8,3,64,128]{3,2,1,0:T(8,128)S(1)}, f32[8,3,64,128]{3,2,1,0:T(8,128)S(1)}, u32[]{:S(2)}, u32[]{:S(2)}) collective-permute-start(f32[8,3,64,128]{3,2,1,0:T(8,128)S(1)} %get-tuple-element.31), channel_id=1, source_target_pairs={{0,1},{1,2},{2,3},{3,4},{4,5},{5,6},{6,7},{8,9},{9,10},{10,11},{11... | collective-permute-start | bytes 2359304 | tf_op jit(solution)/shard_map/ppermute | solution.py:21
  347.1 20.4 %copy-start.9 = (f32[8,8,64,128]{3,2,1,0:T(8,128)S(1)}, f32[8,8,64,128]{3,2,1,0:T(8,128)}, u32[]{:S(2)}) copy-start(f32[8,8,64,128]{3,2,1,0:T(8,128)} %fusion.41) | copy-start | bytes 6291460
  348.8 16.7 %collective-permute-start.14 = (f32[8,3,64,128]{3,2,1,0:T(8,128)S(1)}, f32[8,3,64,128]{3,2,1,0:T(8,128)S(1)}, u32[]{:S(2)}, u32[]{:S(2)}) collective-permute-start(f32[8,3,64,128]{3,2,1,0:T(8,128)S(1)} %get-tuple-element.29), channel_id=1, source_target_pairs={{1,0},{2,1},{3,2},{4,3},{5,4},{6,5},{7,6},{9,8},{10,9},{11,10},{12... | collective-permute-start | bytes 2359304 | tf_op jit(solution)/shard_map/ppermute | solution.py:24
  350.1 16.5 %collective-permute-start.15 = (f32[8,3,64,128]{3,2,1,0:T(8,128)S(1)}, f32[8,3,64,128]{3,2,1,0:T(8,128)S(1)}, u32[]{:S(2)}, u32[]{:S(2)}) collective-permute-start(f32[8,3,64,128]{3,2,1,0:T(8,128)S(1)} %get-tuple-element.28), channel_id=1, source_target_pairs={{0,1},{1,2},{2,3},{3,4},{4,5},{5,6},{6,7},{8,9},{9,10},{10,11},{11... | collective-permute-start | bytes 2359304 | tf_op jit(solution)/shard_map/ppermute | solution.py:21
  (16 other events, 75.9 us)
Sparse Core Ops, SparseCore 0:
  11.2 121.0 all-reduce.11
  315.9 91.5 all-gather.4
  409.2 51.4 all-gather.6
